TPU v7x, 32 devices: a whole 2x2x4 slice. The times are simulated.
32 devices in a mesh: dp: 8 (over z, x), bank: 4 (over y, core).
Axes of the slice: x: 2, y: 2, z: 4, core: 2. Of those that a mesh axis runs over, the one named last changes fastest.
Arguments:
- features: float32 [128, 128], P('dp'), may hold values from -6 to 6
- video_ids: int32 [8, 16], P('dp'), may hold values from 0 to 4, never falling along the last dimension, each value on 1 to 8 neighbouring positions
- bank: float32 [16384, 128], P(('dp', 'bank')), may hold values from -6 to 6
- loss_weight: float32 [128], P('dp'), may hold values from 0.5 to 2
Outputs:
- loss: float32 [128], P('dp')
- feature_grad: float32 [128, 128], P('dp')
Inputs may be any that keep to these rules, and one draw needn't show every extreme that they name: `video_ids`: each row of 16 frames holds 5 videos as runs of equal ids in ascending order, each video 1 to 8 frames and one exactly 8.
All inputs are finite; a program needn't handle non-finite values.
Results may differ from a plain program's by a relative error of at most 0.0003.
Values sent between devices are 32-bit elements; how exact they have to be, the bound alone decides.
A program may use at most 64 MiB of HBM per device.

v0:
```python
import math

import jax
import jax.numpy as jnp
from jax import lax
from jax.sharding import PartitionSpec as P

EPSILON = 1e-06
TAU_BACK = 0.1
HIGHEST = lax.Precision.HIGHEST


def unit_rows(values):
    return values / jnp.sqrt(jnp.sum(values * values, axis=1, keepdims=True) + EPSILON)


def cycle_loss(neighbour, normed, videos):
    frames = videos.shape[0]
    same_video = videos[:, None] == videos[None, :]
    row_index = lax.broadcasted_iota(jnp.int32, (frames, frames), 0)
    col_index = lax.broadcasted_iota(jnp.int32, (frames, frames), 1)
    earlier = same_video & (col_index < row_index)
    position = jnp.sum(jnp.where(earlier, 1.0, 0.0), axis=1).astype(neighbour.dtype)
    products = jnp.dot(neighbour, normed.T, precision=HIGHEST)
    distance = (
        jnp.sum(neighbour * neighbour, axis=1)[:, None]
        - 2.0 * products
        + jnp.sum(normed * normed, axis=1)[None, :]
    )
    back_weight = jnp.where(same_video, jnp.exp(-distance / TAU_BACK), 0.0)
    back_weight = back_weight / jnp.sum(back_weight, axis=1, keepdims=True)
    mean_pos = jnp.dot(back_weight, position, precision=HIGHEST)
    square_pos = jnp.dot(back_weight, position * position, precision=HIGHEST)
    spread = jnp.maximum(square_pos - mean_pos * mean_pos, 1.0)
    return (position - mean_pos) ** 2 / spread + 0.5 * jnp.log(spread)


def reduce_owner(partials):
    whole = lax.psum(partials, "bank")
    return lax.psum_scatter(whole, "dp", scatter_dimension=0, tiled=True)


def shards(features, video_ids, bank, loss_weight):
    per_owner, width = features.shape
    owners = lax.axis_size("dp")
    sharpness = 3.0 * math.sqrt(width)
    lengths = jnp.sqrt(jnp.sum(features * features, axis=1, keepdims=True) + EPSILON)
    normed = features / lengths
    keys = unit_rows(bank)
    gathered = lax.all_gather(normed, "dp", axis=0, tiled=True)
    group = 1
    while owners % (group * 2) == 0 and per_owner * group * 2 <= 512:
        group = group * 2
    step_rows = per_owner * group
    query_blocks = gathered.reshape(-1, step_rows, width)

    def forward_block(query_block):
        exp_scores = jnp.exp(sharpness * jnp.dot(query_block, keys.T, precision=HIGHEST))
        return (jnp.dot(exp_scores, keys, precision=HIGHEST), jnp.sum(exp_scores, axis=1))

    summed, partition = lax.map(forward_block, query_blocks)
    summed, partition = reduce_owner((summed.reshape(-1, width), partition.reshape(-1)))
    neighbour = summed / partition[:, None]
    loss, pullback = jax.vjp(
        lambda soft_rows, unit_part: cycle_loss(soft_rows, unit_part, video_ids[0]),
        neighbour,
        normed,
    )
    grad_soft, grad_local = pullback(loss_weight)
    gathered_grad = lax.all_gather(grad_soft, "dp", axis=0, tiled=True)
    grad_blocks = gathered_grad.reshape(-1, step_rows, width)

    def backward_block(paired):
        query_block, grad_block = paired
        exp_scores = jnp.exp(sharpness * jnp.dot(query_block, keys.T, precision=HIGHEST))
        projected = jnp.dot(grad_block, keys.T, precision=HIGHEST)
        return jnp.dot(exp_scores * projected, keys, precision=HIGHEST)

    moment = lax.map(backward_block, (query_blocks, grad_blocks)).reshape(-1, width)
    moment = reduce_owner((moment,))[0]
    along = jnp.sum(grad_soft * neighbour, axis=1, keepdims=True)
    grad_unit = grad_local + sharpness * (moment / partition[:, None] - along * neighbour)
    feature_grad = (
        grad_unit - normed * jnp.sum(normed * grad_unit, axis=1, keepdims=True)
    ) / lengths
    return (loss, feature_grad)


def solution(mesh):
    return jax.shard_map(
        shards,
        mesh=mesh,
        in_specs=(P("dp", None), P("dp", None), P(("dp", "bank"), None), P("dp")),
        out_specs=(P("dp"), P("dp", None)),
        check_vma=False,
    )
```

profile of v0, /device:TPU:0, one launch (start us, length us, event | category | flops | bytes accessed | tf_op | source)
XLA Modules:
  0.0 221.4 jit_solution(16359548754769475887)
XLA Ops:
  7.2 0.0 reduce-scatter.3.cloned.1.call-start
  7.2 0.8 multiply_reduce_fusion.6
  8.1 1.1 multiply_reduce_fusion
  9.2 0.2 multiply_reduce_fusion.4
  9.4 32.3 %all_gather.6 = f32[128,128]{1,0:T(8,128)S(1)} all-gather(f32[16,128]{1,0:T(8,128)S(1)} %get-tuple-element.42), channel_id=1, replica_groups=mesh['dp'=8,'bank'=4] {'dp'}, dimensions={0}, use_global_device_ids=true | all-gather | bytes 73728 | tf_op jit(solution)/shard_map/all_gather | solution.py:50
  41.7 0.6 fusion.28
  42.3 1.1 fusion.25
  43.4 0.0 reduce-scatter.3.cloned.1.call-update
  43.4 0.0 reduce-scatter.5.cloned.1.call-start
  43.5 0.6 copy-done.4
  44.1 0.6 dynamic-slice.2
  45.3 21.3 %all-reduce = f32[128]{0:T(128)S(1)} all-reduce(f32[128]{0:T(128)S(1)} %get-tuple-element.45), channel_id=3, replica_groups=mesh['dp'=8,'bank'=4] {'dp'}, use_global_device_ids=true, to_apply=%region_7.8.clone | all-reduce | flops 128 | bytes 1024
  66.7 0.1 dynamic-slice.3
  66.7 39.0 %reduce-scatter.3.cloned.1.call-done = f32[16,128]{1,0:T(8,128)} async-done(((f32[128,128]{1,0:T(8,128)}), f32[16,128]{1,0:T(8,128)}) %reduce-scatter.3.cloned.1.call-update) | async-done | bytes 8208 | tf_op jit(solution)/shard_map/reduce_scatter | solution.py:40
  105.7 6.0 %all-reduce.1 = (f32[16,128]{1,0:T(8,128)S(1)}, f32[16]{0:T(128)S(1)}) all-reduce(f32[16,128]{1,0:T(8,128)} %reduce-scatter.3.cloned.1.call-done, f32[16]{0:T(128)S(1)} %dynamic-slice.3), channel_id=1, replica_groups=mesh['dp'=8,'bank'=4] {'bank'}, use_global_device_ids=true, to_apply=%region_3.0 | all-reduce | flops 2064 | bytes 16512 | tf_op jit(solution)/shard_map/psum | solution.py:39
  111.7 0.2 multiply_reduce_fusion.5
  111.9 0.7 copy-done.2
  112.6 0.2 fusion.12
  112.8 0.2 convolution_bitcast_fusion.1
  113.0 0.5 copy-done.3
  113.5 0.7 add_add_fusion
  114.2 0.1 multiply_reduce_fusion.3
  114.3 0.2 multiply_reduce_fusion.8
  114.5 0.3 multiply_reduce_fusion.2
  114.8 30.5 %all_gather.7 = f32[128,128]{1,0:T(8,128)S(1)} all-gather(f32[16,128]{1,0:T(8,128)S(1)} %get-tuple-element.49), channel_id=1, replica_groups=mesh['dp'=8,'bank'=4] {'dp'}, dimensions={0}, use_global_device_ids=true | all-gather | bytes 73728 | tf_op jit(solution)/shard_map/all_gather | solution.py:70
  145.3 0.5 convolution_multiply_fusion
  145.8 1.1 fusion.24
  146.9 0.0 reduce-scatter.5.cloned.1.call-update
  147.0 60.8 %reduce-scatter.5.cloned.1.call-done = f32[16,128]{1,0:T(8,128)} async-done(((f32[128,128]{1,0:T(8,128)}), f32[16,128]{1,0:T(8,128)}) %reduce-scatter.5.cloned.1.call-update) | async-done | bytes 8208 | tf_op jit(solution)/shard_map/reduce_scatter | solution.py:40
  207.7 5.9 %psum.26 = f32[16,128]{1,0:T(8,128)S(1)} all-reduce(f32[16,128]{1,0:T(8,128)} %reduce-scatter.5.cloned.1.call-done), channel_id=1, replica_groups=mesh['dp'=8,'bank'=4] {'bank'}, use_global_device_ids=true, to_apply=%region_14.15 | all-reduce | flops 2048 | bytes 16384 | tf_op jit(solution)/shard_map/psum | solution.py:39
  213.6 0.3 multiply_reduce_fusion.1
  213.9 0.7 subtract_divide_fusion
  (13 shorter events, 0.1 us)
Async XLA Ops:
  7.2 34.5 %copy-start = (f32[512,128]{1,0:T(8,128)S(1)}, f32[512,128]{1,0:T(8,128)}, u32[]{:S(2)}) copy-start(f32[512,128]{1,0:T(8,128)} %param.6) | copy-start | bytes 786436
  7.2 98.6 %reduce-scatter.3.cloned.1.call-start = ((), (), s32[]{:S(2)}) async-start(), calls=%async_computation.2 | async-start | bytes 73728 | tf_op jit(solution)/shard_map/reduce_scatter | solution.py:40
  8.1 1.1 copy-start.1
  43.4 164.3 %reduce-scatter.5.cloned.1.call-start = ((), (), s32[]{:S(2)}) async-start(), calls=%async_computation.3 | async-start | bytes 73728 | tf_op jit(solution)/shard_map/reduce_scatter | solution.py:40
  43.5 0.7 copy-start.4
  111.9 0.7 copy-start.2
  112.8 0.7 copy-start.3
Sparse Core Ops, SparseCore 0:
  43.5 62.1 reduce-scatter.2
  147.1 60.5 reduce-scatter.4
where the time goes:
time: 222 us; the launch traced here: 221 us
  waiting for transfers between devices  99.8 us (45%)
  blocking collectives  95.9 us (43%)
  between operations  14.8 us (7%)
  matrix products  5.06 us (2%)
  other arithmetic  3.32 us (1%)
  local copies, waits for them, and re-layouts  2.43 us (1%)
    reduce_scatter x2, waiting for transfers between devices, reduce_owner(): return lax.psum_scatter(whole, 'dp', scatter_dimension=0, tiled=True)  99.7 us
    all_gather x1, blocking collectives, shards(): gathered = lax.all_gather(normed, 'dp', axis=0, tiled=True)  32.3 us
    all_gather x1, blocking collectives, shards(): gathered_grad = lax.all_gather(grad_soft, 'dp', axis=0, tiled=True)  30.5 us
    unnamed x1, blocking collectives  21.3 us
    psum x2, blocking collectives, reduce_owner(): whole = lax.psum(partials, 'bank')  11.8 us
  transfers between devices with their start and end apart: 2, of which 2 were waited for; matrix products, arithmetic and copies ran while one was open for 0% of the time, Pallas kernels for 0%

commit v1 on v0

v1 whole, which is shorter than its diff:
```python
import functools
import math

import jax
import jax.numpy as jnp
from jax import lax
from jax.experimental import pallas as pl
from jax.experimental.pallas import tpu as pltpu
from jax.sharding import PartitionSpec as P

EPSILON = 1e-06
TAU_BACK = 0.1
HIGHEST = lax.Precision.HIGHEST
MESH = pl.DeviceIdType.MESH
F32, BF16 = jnp.float32, jnp.bfloat16
TILE = 8
NT = (((1,), (1,)), ((), ()))
TN = (((0,), (0,)), ((), ()))
NN = (((1,), (0,)), ((), ()))


def split(values):
    high = values.astype(BF16)
    low = (values - high.astype(F32)).astype(BF16)
    return high, low


def inverse_lengths(values):
    return lax.rsqrt(jnp.sum(values * values, axis=1, keepdims=True) + EPSILON)


def cycle(near, normed, squares, same, pos_row, pos_col, weight):
    products = lax.dot_general(near, normed, NT, precision=HIGHEST, preferred_element_type=F32)
    distance = jnp.sum(near * near, axis=1, keepdims=True) - 2.0 * products + squares
    back = jnp.where(same, jnp.exp(-distance / TAU_BACK), 0.0)
    beta = back / jnp.sum(back, axis=1, keepdims=True)
    mean = jnp.sum(beta * pos_row, axis=1, keepdims=True)
    square = jnp.sum(beta * (pos_row * pos_row), axis=1, keepdims=True)
    variance = square - mean * mean
    spread = jnp.maximum(variance, 1.0)
    off = pos_col - mean
    loss = off * off / spread + 0.5 * jnp.log(spread)
    d_spread = 0.5 / spread - off * off / (spread * spread)
    slope = jnp.where(variance > 1.0, 1.0, jnp.where(variance == 1.0, 0.5, 0.0))
    d_square = d_spread * slope
    d_mean = -2.0 * off / spread - 2.0 * mean * d_square
    d_beta = d_mean * pos_row + d_square * (pos_row * pos_row)
    d_logit = beta * (d_beta - (d_mean * mean + d_square * square))
    return loss, d_logit * weight * (-1.0 / TAU_BACK)


def kernel(
    owners, banks, sharpness,
    feat_ref, ids_ref, bank_ref, weight_ref,
    loss_ref, grad_ref,
    keys_buf, k3, kcat, raw, expo, send1, recv1, tile2, recv2, send3, recv3, tile4, recv4,
    bank_sem, send_sems, recv_sems,
):
    frames, width = feat_ref.shape
    share = frames // banks
    per_tile = TILE // share
    count = owners * banks
    block = min(owners * frames, 128)
    blocks = owners * frames // block
    tiles = block // TILE
    own = lax.axis_index("dp")
    part = lax.axis_index("bank")
    me = own * banks + part

    load = pltpu.make_async_copy(bank_ref, keys_buf, bank_sem)
    load.start()
    barrier = pltpu.get_barrier_semaphore()

    def everyone(body):
        def step(k, carry):
            dst = lax.rem(me + k, count)
            body(dst, (lax.div(dst, banks), lax.rem(dst, banks)))
            return carry
        lax.fori_loop(1, count, step, 0, unroll=count <= 32)

    everyone(lambda dst, where: pl.semaphore_signal(barrier, inc=1, device_id=where, device_id_type=MESH))

    features = feat_ref[...]
    inv_own = inverse_lengths(features)
    normed = features * inv_own
    ones = jnp.ones((TILE, width), F32)
    squares = lax.dot_general(ones, normed * normed, NT, precision=HIGHEST, preferred_element_type=F32)[0:1]
    ids = ids_ref[...].astype(F32)
    weights = weight_ref[...]

    def column(row, first, rows):
        pick = lax.broadcasted_iota(jnp.int32, (rows, frames), 1) == (
            lax.broadcasted_iota(jnp.int32, (rows, frames), 0) + first)
        return jnp.sum(jnp.where(pick, jnp.broadcast_to(row, (rows, frames)), 0.0), axis=1, keepdims=True)

    rows16 = lax.broadcasted_iota(jnp.int32, (frames, frames), 0)
    cols16 = lax.broadcasted_iota(jnp.int32, (frames, frames), 1)
    same_all = column(ids, 0, frames) == ids
    pos_row = jnp.sum(jnp.where(same_all & (rows16 < cols16), 1.0, 0.0), axis=0, keepdims=True)
    pos_all = column(pos_row, 0, frames)
    weight_all = column(weights, 0, frames)
    mine = part * share
    same_mine = column(ids, mine, share) == ids
    pos_mine = column(pos_row, mine, share)
    weight_mine = column(weights, mine, share)

    pl.semaphore_wait(barrier, count - 1)

    def send_features(k, carry):
        dst = lax.rem(own + k, owners)
        pltpu.make_async_remote_copy(
            src_ref=feat_ref, dst_ref=raw.at[own], send_sem=send_sems.at[0], recv_sem=recv_sems.at[0],
            device_id=(dst, part), device_id_type=MESH).start()
        return carry
    lax.fori_loop(1, owners, send_features, 0, unroll=owners <= 8)
    raw[own] = features

    load.wait()
    bank = keys_buf[...]
    key_high, key_low = split(bank * inverse_lengths(bank))
    k3[:, 0:width] = key_high
    k3[:, width:2 * width] = key_high
    k3[:, 2 * width:3 * width] = key_low
    kcat[:, 0:width] = key_high
    kcat[:, width:2 * width] = key_low

    def wait(ref, sem):
        pltpu.make_async_copy(ref, ref, sem).wait()

    wait(raw.at[pl.ds(0, owners - 1)], recv_sems.at[0])

    def project(values):
        high, low = split(values)
        joined = jnp.concatenate([high, low, high], axis=1)
        return lax.dot_general(joined, k3[...], NT, preferred_element_type=F32)

    def collect(values):
        high, low = split(values)
        both = lax.dot_general(high, kcat[...], NN, preferred_element_type=F32)
        rest = lax.dot_general(low, kcat[:, 0:width], NN, preferred_element_type=F32)
        return both[:, 0:width] + (both[:, width:2 * width] + rest)

    group = block // frames

    def forward(index, carry):
        queries = raw[pl.ds(index * group, group)].reshape(block, width)
        queries = queries * inverse_lengths(queries)
        scores = jnp.exp(sharpness * project(queries))
        expo[index] = scores
        summed = collect(scores)
        partition = jnp.broadcast_to(jnp.sum(scores, axis=1, keepdims=True), (block, width))
        base = index * (tiles * per_tile)
        for t in range(tiles * per_tile):
            send1[base + t, 0:share, :] = summed[t * share:(t + 1) * share]
            send1[base + t, share:2 * share, :] = partition[t * share:(t + 1) * share]
        return carry
    if blocks == 1:
        forward(0, 0)
    else:
        lax.fori_loop(0, blocks, forward, 0)

    def spread_out(slot, source, target):
        everyone(lambda dst, where: pltpu.make_async_remote_copy(
            src_ref=source(dst), dst_ref=target.at[me], send_sem=send_sems.at[slot], recv_sem=recv_sems.at[slot],
            device_id=where, device_id_type=MESH).start())

    spread_out(1, lambda dst: send1.at[dst], recv1)
    recv1[me] = send1[me]
    wait(recv1.at[pl.ds(0, count - 1)], recv_sems.at[1])
    total = jnp.sum(recv1[...], axis=0)
    inv_part = 1.0 / total[share:2 * share]
    near = total[0:share] * inv_part
    _, d_dist = cycle(near, normed, squares, same_mine, pos_row, pos_mine, weight_mine)
    grad_soft = 2.0 * (
        near * jnp.sum(d_dist, axis=1, keepdims=True)
        - lax.dot_general(d_dist, normed, NN, precision=HIGHEST, preferred_element_type=F32))

    tile2[...] = jnp.zeros_like(tile2)
    tile2[0:share, :] = grad_soft
    tile2[share:2 * share, :] = near
    spread_out(2, lambda dst: tile2, recv2)
    recv2[me] = tile2[...]
    along = jnp.sum(grad_soft * near, axis=1, keepdims=True)
    wait(recv2.at[pl.ds(0, count - 1)], recv_sems.at[2])

    def backward(index, carry):
        base = index * (tiles * per_tile)
        held = recv2[pl.ds(base, tiles * per_tile)]
        grads = jnp.concatenate([held[t, 0:share] for t in range(tiles * per_tile)], axis=0)
        moment = collect(expo[index] * project(grads))
        for t in range(tiles * per_tile):
            send3[base + t] = moment[t * share:(t + 1) * share]
        return carry
    if blocks == 1:
        backward(0, 0)
    else:
        lax.fori_loop(0, blocks, backward, 0)

    spread_out(3, lambda dst: send3.at[dst], recv3)
    recv3[me] = send3[me]

    first = own * banks
    group_rows = recv2[pl.ds(first, banks)]
    near_all = jnp.concatenate([group_rows[b, share:2 * share] for b in range(banks)], axis=0)
    loss, d_dist_all = cycle(near_all, normed, squares, same_all, pos_row, pos_all, weight_all)
    loss_ref[...] = jnp.sum(jnp.where(rows16 == cols16, jnp.broadcast_to(loss, (frames, frames)), 0.0), axis=0, keepdims=True)
    column_sums = lax.dot_general(d_dist_all, jnp.ones((frames, width), F32), TN, precision=HIGHEST, preferred_element_type=F32)
    grad_local = 2.0 * (
        normed * column_sums
        - lax.dot_general(d_dist_all, near_all, TN, precision=HIGHEST, preferred_element_type=F32))

    wait(recv3.at[pl.ds(0, count - 1)], recv_sems.at[3])
    moment = jnp.sum(recv3[...], axis=0)
    tile4[...] = sharpness * (moment * inv_part - along * near)

    for k in range(1, banks):
        pltpu.make_async_remote_copy(
            src_ref=tile4, dst_ref=recv4.at[part], send_sem=send_sems.at[4], recv_sem=recv_sems.at[4],
            device_id=(own, lax.rem(part + k, banks)), device_id_type=MESH).start()
    recv4[part] = tile4[...]
    wait(recv4.at[pl.ds(0, banks - 1)], recv_sems.at[4])
    held = recv4[...]
    grad_unit = grad_local + jnp.concatenate([held[b] for b in range(banks)], axis=0)
    grad_ref[...] = (grad_unit - normed * jnp.sum(normed * grad_unit, axis=1, keepdims=True)) * inv_own

    wait(raw.at[pl.ds(0, owners - 1)], send_sems.at[0])
    wait(recv1.at[pl.ds(0, count - 1)], send_sems.at[1])
    wait(recv2.at[pl.ds(0, count - 1)], send_sems.at[2])
    wait(recv3.at[pl.ds(0, count - 1)], send_sems.at[3])
    wait(recv4.at[pl.ds(0, banks - 1)], send_sems.at[4])


def shards(owners, banks, features, video_ids, bank, loss_weight):
    frames, width = features.shape
    keys = bank.shape[0]
    count = owners * banks
    share = frames // banks
    block = min(owners * frames, 128)
    blocks = owners * frames // block
    vmem = pl.BlockSpec(memory_space=pltpu.VMEM)
    loss, grad = pl.pallas_call(
        functools.partial(kernel, owners, banks, 3.0 * math.sqrt(width)),
        out_shape=(jax.ShapeDtypeStruct((1, frames), F32), jax.ShapeDtypeStruct((frames, width), F32)),
        in_specs=[vmem, vmem, pl.BlockSpec(memory_space=pl.ANY), vmem],
        out_specs=(vmem, vmem),
        scratch_shapes=[
            pltpu.VMEM((keys, width), F32),
            pltpu.VMEM((keys, 3 * width), BF16),
            pltpu.VMEM((keys, 2 * width), BF16),
            pltpu.VMEM((owners, frames, width), F32),
            pltpu.VMEM((blocks, block, keys), F32),
            pltpu.VMEM((count, TILE, width), F32),
            pltpu.VMEM((count, TILE, width), F32),
            pltpu.VMEM((TILE, width), F32),
            pltpu.VMEM((count, TILE, width), F32),
            pltpu.VMEM((count, share, width), F32),
            pltpu.VMEM((count, share, width), F32),
            pltpu.VMEM((share, width), F32),
            pltpu.VMEM((banks, share, width), F32),
            pltpu.SemaphoreType.DMA,
            pltpu.SemaphoreType.DMA((5,)),
            pltpu.SemaphoreType.DMA((5,)),
        ],
        compiler_params=pltpu.CompilerParams(
            collective_id=0, has_side_effects=True, vmem_limit_bytes=48 * 1024 * 1024),
    )(features, video_ids, bank, loss_weight.reshape(1, frames))
    return loss.reshape(frames), grad


def solution(mesh):
    return jax.shard_map(
        functools.partial(shards, mesh.shape["dp"], mesh.shape["bank"]),
        mesh=mesh,
        in_specs=(P("dp", None), P("dp", None), P(("dp", "bank"), None), P("dp")),
        out_specs=(P("dp"), P("dp", None)),
        check_vma=False,
    )
```

time: 222 us -> 34.8 us (0.16)
  waiting for transfers between devices: 99.8 us -> 0 us
  blocking collectives: 95.9 us -> 0 us
  Pallas kernels: 0 us -> 30.5 us
  between operations: 14.8 us -> 0.66 us
  matrix products: 5.06 us -> 0 us
  other arithmetic: 3.32 us -> 0 us
    reduce_scatter x2 -> x0, waiting for transfers between devices: 99.7 us -> none  [reduce_owner(): return lax.psum_scatter(whole, 'dp', scatter_dimension=0, tiled=True)]
    all_gather x2 -> x0, blocking collectives: 62.8 us -> none  [the longest x1 32.3 us: shards(): gathered = lax.all_gather(normed, 'dp', axis=0, tiled=True)]
    pallas_call x0 -> x1, Pallas kernels: none -> 30.5 us  [shards(): pl.pallas_call(functools.partial(kernel, owners, banks, 3.0 * math.sqrt(w...]
    unnamed x1 -> x0, blocking collectives: 21.3 us -> none
    psum x2 -> x0, blocking collectives: 11.8 us -> none  [reduce_owner(): whole = lax.psum(partials, 'bank')]
    dot_general x9 -> x0, matrix products: 5.06 us -> none  [the longest x1 1.11 us: forward_block(): jnp.dot(exp_scores, keys, precision=HIGHEST)]
    reduce_sum x6 -> x0, other arithmetic: 2.6 us -> none  [the longest x1 1.11 us: unit_rows(): jnp.sum(values * values, axis=1, keepdims=True) + EPSILON]
  transfers between devices with their start and end apart: 2 -> 0, of which waited for: 2 -> 0; matrix products, arithmetic and copies ran while one was open for 0% -> 0% of each run, Pallas kernels for 0% -> 0%
where the time goes in v1:
time: 34.8 us; the launch traced here: 34.5 us
  Pallas kernels  30.5 us (88%)
  local copies, waits for them, and re-layouts  3.41 us (10%)
  between operations  0.66 us (2%)
    pallas_call x1, Pallas kernels, shards(): pl.pallas_call(functools.partial(kernel, owners, banks, 3.0 * math.sqrt(w...  30.5 us
    unnamed x10, local copies, waits for them, and re-layouts  3.41 us

profile of v1, /device:TPU:0, one launch (start us, length us, event | category | flops | bytes accessed | tf_op | source)
XLA Modules:
  0.0 34.5 jit_solution(7585137097590177775)
XLA Ops:
  0.6 0.0 copy-start.3
  0.6 0.0 copy-start.2
  0.7 0.6 %copy-done.3 = f32[16]{0:T(128)S(1)} copy-done((f32[16]{0:T(128)S(1)}, f32[16]{0:T(128)}, u32[]{:S(2)}) %copy-start.3) | copy-done | bytes 88
  1.3 0.0 copy-done.2
  1.3 0.0 copy-start
  1.3 0.9 %copy-done = f32[512,128]{1,0:T(8,128)S(1)} copy-done((f32[512,128]{1,0:T(8,128)S(1)}, f32[512,128]{1,0:T(8,128)}, u32[]{:S(2)}) %copy-start) | copy-done | bytes 262168
  2.3 0.0 copy-start.1
  2.3 0.7 %copy-done.1 = f32[16,128]{1,0:T(8,128)S(1)} copy-done((f32[16,128]{1,0:T(8,128)S(1)}, f32[16,128]{1,0:T(8,128)}, u32[]{:S(2)}) %copy-start.1) | copy-done | bytes 8216
  3.0 30.5 %shard_map.59 = (f32[1,16]{1,0:T(1,128)S(1)}, f32[16,128]{1,0:T(8,128)S(1)}) custom-call(f32[16,128]{1,0:T(8,128)S(1)} %copy-done.1, s32[1,16]{1,0:T(1,128)S(1)} %copy-done.2, f32[512,128]{1,0:T(8,128)S(1)} %copy-done, f32[1,16]{1,0:T(1,128)S(1)} %bitcast.2), custom_call_target="tpu_custom_call" | custom-call | tf_op jit(solution)/shard_map/pallas_call | solution.py:241
  33.4 0.5 %copy.8 = f32[16]{0:T(128)} copy(f32[16]{0:T(128)S(1)} %bitcast.3) | data formatting | bytes 128
  33.9 0.6 %copy.9 = f32[16,128]{1,0:T(8,128)} copy(f32[16,128]{1,0:T(8,128)S(1)} %get-tuple-element.9) | data formatting | bytes 16384
Async XLA Ops:
  0.6 0.7 %copy-start.3 = (f32[16]{0:T(128)S(1)}, f32[16]{0:T(128)}, u32[]{:S(2)}) copy-start(f32[16]{0:T(128)} %param.7) | copy-start | bytes 196
  0.6 0.7 %copy-start.2 = (s32[1,16]{1,0:T(1,128)S(1)}, s32[1,16]{1,0:T(1,128)}, u32[]{:S(2)}) copy-start(s32[1,16]{1,0:T(1,128)} %ids_ref.1) | copy-start | bytes 196
  1.3 0.9 %copy-start = (f32[512,128]{1,0:T(8,128)S(1)}, f32[512,128]{1,0:T(8,128)}, u32[]{:S(2)}) copy-start(f32[512,128]{1,0:T(8,128)} %bank_ref.1) | copy-start | bytes 786436
  2.3 0.7 %copy-start.1 = (f32[16,128]{1,0:T(8,128)S(1)}, f32[16,128]{1,0:T(8,128)}, u32[]{:S(2)}) copy-start(f32[16,128]{1,0:T(8,128)} %feat_ref.1) | copy-start | bytes 24580

commit v2 on v1

v2 whole, which is shorter than its diff:
```python
import functools
import math

import jax
import jax.numpy as jnp
from jax import lax
from jax.experimental import pallas as pl
from jax.experimental.pallas import tpu as pltpu
from jax.sharding import PartitionSpec as P

EPSILON = 1e-06
TAU_BACK = 0.1
HIGHEST = lax.Precision.HIGHEST
MESH = pl.DeviceIdType.MESH
F32, BF16 = jnp.float32, jnp.bfloat16
TILE = 8
NT = (((1,), (1,)), ((), ()))
TN = (((0,), (0,)), ((), ()))
NN = (((1,), (0,)), ((), ()))


def split(values):
    high = values.astype(BF16)
    low = (values - high.astype(F32)).astype(BF16)
    return high, low


def inverse_lengths(values):
    return lax.rsqrt(jnp.sum(values * values, axis=1, keepdims=True) + EPSILON)


def cycle(near, normed, squares, same, pos_row, pos_col, weight):
    products = lax.dot_general(near, normed, NT, precision=HIGHEST, preferred_element_type=F32)
    norms = jnp.sum(near * near, axis=1, keepdims=True)
    distance = norms - 2.0 * products + squares
    back = jnp.where(same, jnp.exp(-distance / TAU_BACK), 0.0)
    beta = back / jnp.sum(back, axis=1, keepdims=True)
    mean = jnp.sum(beta * pos_row, axis=1, keepdims=True)
    square = jnp.sum(beta * (pos_row * pos_row), axis=1, keepdims=True)
    variance = square - mean * mean
    spread = jnp.maximum(variance, 1.0)
    off = pos_col - mean
    loss = off * off / spread + 0.5 * jnp.log(spread)
    d_spread = 0.5 / spread - off * off / (spread * spread)
    slope = jnp.where(variance > 1.0, 1.0, jnp.where(variance == 1.0, 0.5, 0.0))
    d_square = d_spread * slope
    d_mean = -2.0 * off / spread - 2.0 * mean * d_square
    d_beta = d_mean * pos_row + d_square * (pos_row * pos_row)
    d_logit = beta * (d_beta - (d_mean * mean + d_square * square))
    d_dist = d_logit * weight * (-1.0 / TAU_BACK)
    along = 2.0 * jnp.sum(d_dist * (norms - products), axis=1, keepdims=True)
    return loss, d_dist, along


def kernel(
    owners, banks, sharpness,
    feat_hbm, ids_hbm, bank_ref, weight_hbm,
    loss_ref, grad_ref,
    feat_ref, ids_ref, weight_ref, keys_buf, k3, kcat, out0, raw, score, expo,
    send1, recvx, recv1, tile4, recv4,
    load_sems, send_sems, recv_sems,
):
    frames, width = feat_hbm.shape
    share = frames // banks
    halves = banks // 2
    cells = owners * halves
    folds = frames // TILE
    block = min(owners * frames, 128)
    blocks = owners * frames // block
    group = block // frames
    own = lax.axis_index("dp")
    part = lax.axis_index("bank")
    side = lax.rem(part, 2)
    twin = part + 1 - 2 * side
    cell = own * halves + lax.div(part, 2)

    loads = [
        pltpu.make_async_copy(feat_hbm, feat_ref, load_sems.at[0]),
        pltpu.make_async_copy(bank_ref, keys_buf, load_sems.at[1]),
        pltpu.make_async_copy(ids_hbm, ids_ref, load_sems.at[2]),
        pltpu.make_async_copy(weight_hbm, weight_ref, load_sems.at[3]),
    ]
    for load in loads:
        load.start()
    barrier = pltpu.get_barrier_semaphore()

    def every_cell(body):
        def step(k, carry):
            dst = lax.rem(cell + k, cells)
            body(dst, (lax.div(dst, halves), 2 * lax.rem(dst, halves) + side))
            return carry
        lax.fori_loop(1, cells, step, 0, unroll=cells <= 16)

    every_cell(lambda dst, where: pl.semaphore_signal(barrier, inc=1, device_id=where, device_id_type=MESH))
    for k in range(1, banks, 2):
        pl.semaphore_signal(barrier, inc=1, device_id=(own, lax.rem(part + k, banks)), device_id_type=MESH)

    for index in (0, 2, 3):
        loads[index].wait()
    features = feat_ref[...]
    inv_own = inverse_lengths(features)
    normed = features * inv_own
    ones = jnp.ones((TILE, width), F32)
    squares = lax.dot_general(ones, normed * normed, NT, precision=HIGHEST, preferred_element_type=F32)[0:1]
    ids = ids_ref[...].astype(F32)
    weights = weight_ref[...]

    def column(row, first, rows):
        pick = lax.broadcasted_iota(jnp.int32, (rows, frames), 1) == (
            lax.broadcasted_iota(jnp.int32, (rows, frames), 0) + first)
        return jnp.sum(jnp.where(pick, jnp.broadcast_to(row, (rows, frames)), 0.0), axis=1, keepdims=True)

    rows16 = lax.broadcasted_iota(jnp.int32, (frames, frames), 0)
    cols16 = lax.broadcasted_iota(jnp.int32, (frames, frames), 1)
    same_all = column(ids, 0, frames) == ids
    pos_row = jnp.sum(jnp.where(same_all & (rows16 < cols16), 1.0, 0.0), axis=0, keepdims=True)
    mine = part * share
    same_mine = column(ids, mine, share) == ids
    pos_mine = column(pos_row, mine, share)
    weight_mine = column(weights, mine, share)

    out0[0:frames, :] = features
    out0[frames:2 * frames, :] = jnp.zeros((frames, width), F32)
    out0[frames:2 * frames, 0:frames] = jnp.where(same_all, 1.0, 0.0)

    pl.semaphore_wait(barrier, cells - 1 + halves)

    def send_features(k, carry):
        dst = lax.rem(own + k, owners)
        pltpu.make_async_remote_copy(
            src_ref=out0, dst_ref=raw.at[own], send_sem=send_sems.at[0], recv_sem=recv_sems.at[0],
            device_id=(dst, part), device_id_type=MESH).start()
        return carry
    lax.fori_loop(1, owners, send_features, 0, unroll=owners <= 8)
    raw[own] = out0[...]

    loads[1].wait()
    bank = keys_buf[...]
    key_high, key_low = split(bank * inverse_lengths(bank))
    k3[:, 0:width] = key_high
    k3[:, width:2 * width] = key_high
    k3[:, 2 * width:3 * width] = key_low
    kcat[:, 0:width] = key_high
    kcat[:, width:2 * width] = key_low

    def wait(ref, sem):
        pltpu.make_async_copy(ref, ref, sem).wait()

    def project(values):
        high, low = split(values)
        joined = jnp.concatenate([high, low, high], axis=1)
        return lax.dot_general(joined, k3[...], NT, preferred_element_type=F32)

    def collect(values):
        high, low = split(values)
        both = lax.dot_general(high, kcat[...], NN, preferred_element_type=F32)
        rest = lax.dot_general(low, kcat[:, 0:width], NN, preferred_element_type=F32)
        return both[:, 0:width] + (both[:, width:2 * width] + rest)

    def each(count, body):
        if count <= 8:
            for k in range(count):
                body(k)
        else:
            lax.fori_loop(0, count, lambda k, carry: (body(k), carry)[1], 0)

    wait(raw.at[pl.ds(0, owners - 1)], recv_sems.at[0])

    def forward(index):
        queries = raw[pl.ds(index * group, group), 0:frames].reshape(block, width)
        scores = project(queries * inverse_lengths(queries))
        weighted = jnp.exp(sharpness * scores)
        score[...] = scores
        expo[...] = weighted
        summed = collect(weighted)
        partition = jnp.broadcast_to(jnp.sum(weighted, axis=1, keepdims=True), (block, width))
        for g in range(group):
            owner = index * group + g
            shared = raw[owner, frames:2 * frames, 0:frames]
            for b in range(banks):
                spot = send1.at[b % 2, owner * halves + b // 2]
                row = g * frames + b * share
                spot[0:share, :] = summed[row:row + share]
                spot[share:2 * share, :] = partition[row:row + share]
            pairs = []
            for i in range(frames):
                picked = None
                for f in range(folds):
                    term = shared[f * TILE:(f + 1) * TILE, i:i + 1] * score[pl.ds(g * frames + f * TILE, TILE), :]
                    picked = term if picked is None else picked + term
                pairs.append(picked * expo[pl.ds(g * frames + i, 1), :])
            second = collect(jnp.concatenate(pairs, axis=0))
            for i in range(frames):
                b = i // share
                first = TILE + (i % share) * TILE
                send1[b % 2, owner * halves + b // 2, first:first + TILE, :] = second[i * TILE:(i + 1) * TILE]
    each(blocks, forward)

    pltpu.make_async_remote_copy(
        src_ref=send1.at[1 - side], dst_ref=recvx, send_sem=send_sems.at[1], recv_sem=recv_sems.at[1],
        device_id=(own, twin), device_id_type=MESH).start()
    wait(recvx, recv_sems.at[1])
    send1[side] = send1[side] + recvx[...]

    every_cell(lambda dst, where: pltpu.make_async_remote_copy(
        src_ref=send1.at[side, dst], dst_ref=recv1.at[cell], send_sem=send_sems.at[2], recv_sem=recv_sems.at[2],
        device_id=where, device_id_type=MESH).start())
    recv1[cell] = send1[side, cell]
    wait(recv1.at[pl.ds(0, cells - 1)], recv_sems.at[2])
    total = jnp.sum(recv1[...], axis=0)
    inv_part = 1.0 / total[share:2 * share]
    near = total[0:share] * inv_part
    loss, d_dist, along = cycle(near, normed, squares, same_mine, pos_row, pos_mine, weight_mine)
    pairs = share * TILE
    fold = jnp.where(
        lax.rem(lax.broadcasted_iota(jnp.int32, (frames, pairs), 0), TILE)
        == lax.rem(lax.broadcasted_iota(jnp.int32, (frames, pairs), 1), TILE), -2.0, 0.0)
    factors = lax.dot_general(d_dist, fold, NN, precision=HIGHEST, preferred_element_type=F32)
    factors = jnp.where(
        lax.div(lax.broadcasted_iota(jnp.int32, (share, pairs), 1), TILE)
        == lax.broadcasted_iota(jnp.int32, (share, pairs), 0), factors, 0.0)
    moment = lax.dot_general(factors, total[TILE:TILE + pairs], NN, precision=HIGHEST, preferred_element_type=F32)
    rows = sharpness * (moment * inv_part - along * near)
    joined = jnp.concatenate([near, jnp.ones((share, width), F32)], axis=1)
    local = lax.dot_general(d_dist, joined, TN, precision=HIGHEST, preferred_element_type=F32)
    local = 2.0 * (normed * local[:, width:2 * width] - local[:, 0:width])
    placed = jnp.concatenate([rows] * banks, axis=0)
    is_mine = lax.div(lax.broadcasted_iota(jnp.int32, (frames, width), 0), share) == part
    tile4[0:frames, :] = local + jnp.where(is_mine, placed, 0.0)
    tile4[frames:frames + TILE, :] = jnp.zeros((TILE, width), F32)
    tile4[frames:frames + share, :] = jnp.broadcast_to(loss, (share, width))

    for k in range(1, banks):
        pltpu.make_async_remote_copy(
            src_ref=tile4, dst_ref=recv4.at[part], send_sem=send_sems.at[3], recv_sem=recv_sems.at[3],
            device_id=(own, lax.rem(part + k, banks)), device_id_type=MESH).start()
    recv4[part] = tile4[...]
    wait(raw.at[pl.ds(0, owners - 1)], send_sems.at[0])
    wait(recvx, send_sems.at[1])
    wait(recv1.at[pl.ds(0, cells - 1)], send_sems.at[2])
    wait(recv4.at[pl.ds(0, banks - 1)], recv_sems.at[3])
    held = recv4[...]
    grad_unit = jnp.sum(held[:, 0:frames], axis=0)
    grad_ref[...] = (grad_unit - normed * jnp.sum(normed * grad_unit, axis=1, keepdims=True)) * inv_own
    losses = jnp.concatenate([held[b, frames:frames + share] for b in range(banks)], axis=0)[:, 0:frames]
    loss_ref[...] = jnp.sum(jnp.where(rows16 == cols16, losses, 0.0), axis=0, keepdims=True)
    wait(recv4.at[pl.ds(0, banks - 1)], send_sems.at[3])


def shards(owners, banks, features, video_ids, bank, loss_weight):
    frames, width = features.shape
    keys = bank.shape[0]
    cells = owners * banks // 2
    message = TILE + frames // banks * TILE
    block = min(owners * frames, 128)
    vmem = pl.BlockSpec(memory_space=pltpu.VMEM)
    loss, grad = pl.pallas_call(
        functools.partial(kernel, owners, banks, 3.0 * math.sqrt(width)),
        out_shape=(jax.ShapeDtypeStruct((1, frames), F32), jax.ShapeDtypeStruct((frames, width), F32)),
        in_specs=[pl.BlockSpec(memory_space=pltpu.HBM)] * 4,
        out_specs=(vmem, vmem),
        scratch_shapes=[
            pltpu.VMEM((frames, width), F32),
            pltpu.VMEM((1, frames), jnp.int32),
            pltpu.VMEM((1, frames), F32),
            pltpu.VMEM((keys, width), F32),
            pltpu.VMEM((keys, 3 * width), BF16),
            pltpu.VMEM((keys, 2 * width), BF16),
            pltpu.VMEM((2 * frames, width), F32),
            pltpu.VMEM((owners, 2 * frames, width), F32),
            pltpu.VMEM((block, keys), F32),
            pltpu.VMEM((block, keys), F32),
            pltpu.VMEM((2, cells, message, width), F32),
            pltpu.VMEM((cells, message, width), F32),
            pltpu.VMEM((cells, message, width), F32),
            pltpu.VMEM((frames + TILE, width), F32),
            pltpu.VMEM((banks, frames + TILE, width), F32),
            pltpu.SemaphoreType.DMA((4,)),
            pltpu.SemaphoreType.DMA((4,)),
            pltpu.SemaphoreType.DMA((4,)),
        ],
        compiler_params=pltpu.CompilerParams(
            collective_id=0, has_side_effects=True, vmem_limit_bytes=60 * 1024 * 1024),
    )(features, video_ids, bank, loss_weight.reshape(1, frames))
    return loss.reshape(frames), grad


def solution(mesh):
    return jax.shard_map(
        functools.partial(shards, mesh.shape["dp"], mesh.shape["bank"]),
        mesh=mesh,
        in_specs=(P("dp", None), P("dp", None), P(("dp", "bank"), None), P("dp")),
        out_specs=(P("dp"), P("dp", None)),
        check_vma=False,
    )
```

time: 34.8 us -> 27.7 us (0.80)
  Pallas kernels: 30.5 us -> 24.3 us
  local copies, waits for them, and re-layouts: 3.41 us -> 2.47 us
    pallas_call x1, Pallas kernels: 30.5 us -> 24.3 us  [shards(): pl.pallas_call(functools.partial(kernel, owners, banks, 3.0 * math.sqrt(w...]
    unnamed x10 -> x4, local copies, waits for them, and re-layouts: 3.41 us -> 2.47 us
where the time goes in v2:
time: 27.7 us; the launch traced here: 27.4 us
  Pallas kernels  24.3 us (88%)
  local copies, waits for them, and re-layouts  2.47 us (9%)
  between operations  0.65 us (2%)
    pallas_call x1, Pallas kernels, shards(): pl.pallas_call(functools.partial(kernel, owners, banks, 3.0 * math.sqrt(w...  24.3 us
    unnamed x4, local copies, waits for them, and re-layouts  2.47 us

profile of v2, /device:TPU:0, one launch (start us, length us, event | category | flops | bytes accessed | tf_op | source)
XLA Modules:
  0.0 27.4 jit_solution(8481990044957741290)
XLA Ops:
  0.6 24.3 %shard_map.59 = (f32[1,16]{1,0:T(1,128)}, f32[16,128]{1,0:T(8,128)}) custom-call(f32[16,128]{1,0:T(8,128)} %feat_hbm.1, s32[1,16]{1,0:T(1,128)} %ids_hbm.1, f32[512,128]{1,0:T(8,128)} %bank_ref.1, f32[1,16]{1,0:T(1,128)} %bitcast.2), custom_call_target="tpu_custom_call" | custom-call | tf_op jit(solution)/shard_map/pallas_call | solution.py:257
  24.9 0.0 copy-start
  24.9 0.7 %copy-done = f32[1,16]{1,0:T(1,128)S(1)} copy-done((f32[1,16]{1,0:T(1,128)S(1)}, f32[1,16]{1,0:T(1,128)}, u32[]{:S(2)}) %copy-start) | copy-done | bytes 88
  25.6 0.5 %copy.8 = f32[16]{0:T(128)} copy(f32[16]{0:T(128)S(1)} %bitcast.3) | data formatting | bytes 128
  26.1 1.3 %copy.9 = f32[16,128]{1,0:T(8,128)} copy(f32[16,128]{1,0:T(8,128)} %get-tuple-element.9) | data formatting | bytes 16384
Async XLA Ops:
  24.9 0.7 %copy-start = (f32[1,16]{1,0:T(1,128)S(1)}, f32[1,16]{1,0:T(1,128)}, u32[]{:S(2)}) copy-start(f32[1,16]{1,0:T(1,128)} %get-tuple-element.4) | copy-start | bytes 196

commit v3 on v2

--- a/solution.py
+++ b/solution.py
@@ -68,6 +68,9 @@
     block = min(owners * frames, 128)
     blocks = owners * frames // block
     group = block // frames
+    pairs_rows = share * TILE
+    sent = pairs_rows + share + 1
+    lane_pick = lax.broadcasted_iota(jnp.int32, (share, width), 1) == lax.broadcasted_iota(jnp.int32, (share, width), 0)
     own = lax.axis_index("dp")
     part = lax.axis_index("bank")
     side = lax.rem(part, 2)
@@ -180,8 +183,8 @@
             for b in range(banks):
                 spot = send1.at[b % 2, owner * halves + b // 2]
                 row = g * frames + b * share
-                spot[0:share, :] = summed[row:row + share]
-                spot[share:2 * share, :] = partition[row:row + share]
+                spot[pairs_rows:pairs_rows + share, :] = summed[row:row + share]
+                spot[pairs_rows + share:sent, :] = jnp.sum(jnp.where(lane_pick, partition[row:row + share], 0.0), axis=0, keepdims=True)
             pairs = []
             for i in range(frames):
                 picked = None
@@ -192,24 +195,25 @@
             second = collect(jnp.concatenate(pairs, axis=0))
             for i in range(frames):
                 b = i // share
-                first = TILE + (i % share) * TILE
+                first = (i % share) * TILE
                 send1[b % 2, owner * halves + b // 2, first:first + TILE, :] = second[i * TILE:(i + 1) * TILE]
     each(blocks, forward)
 
     pltpu.make_async_remote_copy(
-        src_ref=send1.at[1 - side], dst_ref=recvx, send_sem=send_sems.at[1], recv_sem=recv_sems.at[1],
+        src_ref=send1.at[1 - side, :, 0:sent], dst_ref=recvx.at[:, 0:sent], send_sem=send_sems.at[1], recv_sem=recv_sems.at[1],
         device_id=(own, twin), device_id_type=MESH).start()
-    wait(recvx, recv_sems.at[1])
-    send1[side] = send1[side] + recvx[...]
+    wait(recvx.at[:, 0:sent], recv_sems.at[1])
+    send1[side, :, 0:sent] = send1[side, :, 0:sent] + recvx[:, 0:sent]
 
     every_cell(lambda dst, where: pltpu.make_async_remote_copy(
-        src_ref=send1.at[side, dst], dst_ref=recv1.at[cell], send_sem=send_sems.at[2], recv_sem=recv_sems.at[2],
+        src_ref=send1.at[side, dst, 0:sent], dst_ref=recv1.at[cell, 0:sent], send_sem=send_sems.at[2], recv_sem=recv_sems.at[2],
         device_id=where, device_id_type=MESH).start())
-    recv1[cell] = send1[side, cell]
-    wait(recv1.at[pl.ds(0, cells - 1)], recv_sems.at[2])
-    total = jnp.sum(recv1[...], axis=0)
-    inv_part = 1.0 / total[share:2 * share]
-    near = total[0:share] * inv_part
+    recv1[cell, 0:sent] = send1[side, cell, 0:sent]
+    wait(recv1.at[pl.ds(0, cells - 1), 0:sent], recv_sems.at[2])
+    total = jnp.sum(recv1[:, 0:sent], axis=0)
+    parts = jnp.broadcast_to(total[pairs_rows + share:sent], (share, width))
+    inv_part = 1.0 / jnp.sum(jnp.where(lane_pick, parts, 0.0), axis=1, keepdims=True)
+    near = total[pairs_rows:pairs_rows + share] * inv_part
     loss, d_dist, along = cycle(near, normed, squares, same_mine, pos_row, pos_mine, weight_mine)
     pairs = share * TILE
     fold = jnp.where(
@@ -219,7 +223,7 @@
     factors = jnp.where(
         lax.div(lax.broadcasted_iota(jnp.int32, (share, pairs), 1), TILE)
         == lax.broadcasted_iota(jnp.int32, (share, pairs), 0), factors, 0.0)
-    moment = lax.dot_general(factors, total[TILE:TILE + pairs], NN, precision=HIGHEST, preferred_element_type=F32)
+    moment = lax.dot_general(factors, total[0:pairs], NN, precision=HIGHEST, preferred_element_type=F32)
     rows = sharpness * (moment * inv_part - along * near)
     joined = jnp.concatenate([near, jnp.ones((share, width), F32)], axis=1)
     local = lax.dot_general(d_dist, joined, TN, precision=HIGHEST, preferred_element_type=F32)
@@ -236,8 +240,8 @@
             device_id=(own, lax.rem(part + k, banks)), device_id_type=MESH).start()
     recv4[part] = tile4[...]
     wait(raw.at[pl.ds(0, owners - 1)], send_sems.at[0])
-    wait(recvx, send_sems.at[1])
-    wait(recv1.at[pl.ds(0, cells - 1)], send_sems.at[2])
+    wait(recvx.at[:, 0:sent], send_sems.at[1])
+    wait(recv1.at[pl.ds(0, cells - 1), 0:sent], send_sems.at[2])
     wait(recv4.at[pl.ds(0, banks - 1)], recv_sems.at[3])
     held = recv4[...]
     grad_unit = jnp.sum(held[:, 0:frames], axis=0)

time: 27.7 us -> 27.3 us (0.986)
  Pallas kernels: 24.3 us -> 23.9 us
    pallas_call x1, Pallas kernels: 24.3 us -> 23.9 us  [shards(): pl.pallas_call(functools.partial(kernel, owners, banks, 3.0 * math.sqrt(w...]
where the time goes in v3:
time: 27.3 us; the launch traced here: 27 us
  Pallas kernels  23.9 us (88%)
  local copies, waits for them, and re-layouts  2.47 us (9%)
  between operations  0.65 us (2%)
    pallas_call x1, Pallas kernels, shards(): pl.pallas_call(functools.partial(kernel, owners, banks, 3.0 * math.sqrt(w...  23.9 us
    unnamed x4, local copies, waits for them, and re-layouts  2.47 us

profile of v3, /device:TPU:0, one launch (start us, length us, event | category | flops | bytes accessed | tf_op | source)
XLA Modules:
  0.0 27.0 jit_solution(3529475553848782819)
XLA Ops:
  0.6 23.9 %shard_map.59 = (f32[1,16]{1,0:T(1,128)}, f32[16,128]{1,0:T(8,128)}) custom-call(f32[16,128]{1,0:T(8,128)} %feat_hbm.1, s32[1,16]{1,0:T(1,128)} %ids_hbm.1, f32[512,128]{1,0:T(8,128)} %bank_ref.1, f32[1,16]{1,0:T(1,128)} %bitcast.2), custom_call_target="tpu_custom_call" | custom-call | tf_op jit(solution)/shard_map/pallas_call | solution.py:261
  24.6 0.0 copy-start
  24.6 0.7 %copy-done = f32[1,16]{1,0:T(1,128)S(1)} copy-done((f32[1,16]{1,0:T(1,128)S(1)}, f32[1,16]{1,0:T(1,128)}, u32[]{:S(2)}) %copy-start) | copy-done | bytes 88
  25.2 0.5 %copy.8 = f32[16]{0:T(128)} copy(f32[16]{0:T(128)S(1)} %bitcast.3) | data formatting | bytes 128
  25.7 1.3 %copy.9 = f32[16,128]{1,0:T(8,128)} copy(f32[16,128]{1,0:T(8,128)} %get-tuple-element.9) | data formatting | bytes 16384
Async XLA Ops:
  24.6 0.7 %copy-start = (f32[1,16]{1,0:T(1,128)S(1)}, f32[1,16]{1,0:T(1,128)}, u32[]{:S(2)}) copy-start(f32[1,16]{1,0:T(1,128)} %get-tuple-element.4) | copy-start | bytes 196
